TPU v7x, 32 devices: a whole 2x2x4 slice. The times are simulated.
32 devices in a mesh: dp: 4 (over y, x), mp: 8 (over z, core).
Axes of the slice: x: 2, y: 2, z: 4, core: 2. Of those that a mesh axis runs over, the one named last changes fastest.
Arguments:
- activations: bfloat16 [4096, 2048], P('dp', 'mp'), may hold values from -6 to 6
- out_grad: bfloat16 [4096, 8192], P('dp'), may hold values from -0.8984375 to 0.8984375
- old_weight: bfloat16 [8, 256, 8192], P('mp', 'dp'), may hold values from -0.125 to 0.125
- old_first: float32 [8, 256, 8192], P('mp', 'dp'), may hold values from -6 to 6
- old_second: float32 [8, 256, 8192], P('mp', 'dp'), may hold values from 0.25 to 4
- step: int32 [1], replicated, may hold values from 1 to 31
- next_input: bfloat16 [4096, 2048], P('dp', 'mp'), may hold values from -6 to 6
Outputs:
- new_weight: bfloat16 [8, 344, 8192], P('mp', 'dp')
- new_first: float32 [8, 344, 8192], P('mp', 'dp')
- new_second: float32 [8, 344, 8192], P('mp', 'dp')
- output: bfloat16 [4096, 8192], P('dp', 'mp')
Inputs may be any that keep to these rules, and one draw needn't show every extreme that they name: `step`: the number of Adam steps taken, this one included.
All inputs are finite; a program needn't handle non-finite values.
Results may differ from a plain program's by a relative error of at most 0.0049.
Values may be sent and summed in bfloat16 or wider, within the bound.
A program may use at most 192 MiB of HBM per device.

v0:
```python
import jax
import jax.numpy as jnp
from jax import lax
from jax.sharding import PartitionSpec as P


def partner(i, k, n):
    return i ^ k if n & n - 1 == 0 else (i + k) % n


def exchange(block, axis, k):
    n = lax.axis_size(axis)
    return lax.ppermute(block, axis, [(i, partner(i, k, n)) for i in range(n)])


def target(k, n, axis):
    me = lax.axis_index(axis)
    return me ^ k if n & n - 1 == 0 else lax.rem(me + k, n)


def to_front(block, axis):
    n = lax.axis_size(axis)
    return lax.ppermute(block, axis, [(i, i - 1) for i in range(1, n)])


def body(activations, out_grad, old_weight, old_first, old_second, step, next_input):
    owners = lax.axis_size("dp")
    owner = lax.axis_index("dp")
    old_rows = old_weight.shape[1]
    width = old_weight.shape[2]
    held_rows = old_rows * owners
    shard_rows = (held_rows + owners - 2) // (owners - 1)
    input_all = lax.all_gather(next_input, "mp", axis=1, tiled=True)
    part = lax.dot_general(
        activations, out_grad, (((0,), (0,)), ((), ())), preferred_element_type=jnp.float32
    ).astype(jnp.bfloat16)
    part = part.reshape(owners, old_rows, width)
    grad = lax.dynamic_index_in_dim(part, owner, 0, keepdims=False).astype(jnp.float32)
    for k in range(1, owners):
        away = lax.dynamic_index_in_dim(part, target(k, owners, "dp"), 0, keepdims=False)
        grad = grad + exchange(away, "dp", k).astype(jnp.float32)
    step_float = step[0].astype(jnp.float32)
    first_fix = 1.0 - jnp.power(jnp.float32(0.9), step_float)
    second_fix = 1.0 - jnp.power(jnp.float32(0.95), step_float)
    new_first = 0.9 * old_first[0] + 0.1 * grad
    new_second = 0.95 * old_second[0] + 0.05 * grad * grad
    update = new_first / first_fix / (jnp.sqrt(new_second / second_fix) + 1e-08)
    new_weight = (old_weight[0].astype(jnp.float32) - 0.01 * update).astype(jnp.bfloat16)
    weight_part = lax.all_to_all(new_weight, "mp", split_axis=1, concat_axis=0, tiled=True)
    heads = lax.axis_size("mp")
    weight_part = weight_part.reshape(heads, old_rows, -1)
    weight_cols = lax.all_gather(weight_part, "dp", axis=1, tiled=True)
    weight_cols = weight_cols.reshape(heads * held_rows, -1)
    begin = owner * (shard_rows - old_rows)

    def mine(block):
        behind = to_front(block.astype(jnp.bfloat16), "dp").astype(block.dtype)
        rows = jnp.concatenate([block, behind, jnp.zeros((shard_rows, width), block.dtype)], 0)
        return lax.dynamic_slice_in_dim(rows, begin, shard_rows, 0)[None]

    outs = (mine(new_weight), mine(new_first), mine(new_second))
    output = jnp.dot(input_all, weight_cols, preferred_element_type=jnp.float32).astype(
        jnp.bfloat16
    )
    return (*outs, output)


def solution(mesh):
    return jax.shard_map(
        body,
        mesh=mesh,
        in_specs=(
            P("dp", "mp"),
            P("dp", None),
            P("mp", "dp", None),
            P("mp", "dp", None),
            P("mp", "dp", None),
            P(),
            P("dp", "mp"),
        ),
        out_specs=(P("mp", "dp", None), P("mp", "dp", None), P("mp", "dp", None), P("dp", "mp")),
        check_vma=False,
    )
```

profile of v0, /device:TPU:0, one launch (start us, length us, event | category | flops | bytes accessed | tf_op | source)
XLA Modules:
  0.0 292.9 jit_solution(17170010049314651664)
XLA Ops:
  7.2 1.0 copy-done
  8.2 10.7 %convolution_convert_fusion = bf16[256,8192]{1,0:T(8,128)(2,1)S(1)} fusion(bf16[1024,256]{1,0:T(8,128)(2,1)S(1)} %copy-done, bf16[1024,8192]{1,0:T(8,128)(2,1)} %param.8), kind=kOutput, calls=%fused_computation | convolution fusion | flops 4297064448 | bytes 21495808 | tf_op jit(solution)/shard_map/dot_general | solution.py:34
  19.0 1.8 dynamic-slice_bitcast_fusion.2
  20.7 1.2 copy-done.4
  21.9 2.9 %collective-permute-start = (bf16[64,8192]{1,0:T(8,128)(2,1)}, bf16[64,8192]{1,0:T(8,128)(2,1)S(1)}, u32[]{:S(2)}, u32[]{:S(2)}) collective-permute-start(bf16[64,8192]{1,0:T(8,128)(2,1)} %get-tuple-element.26), channel_id=1, source_target_pairs={{0,8},{8,0},{16,24},{24,16},{1,9},{9,1},{17,25},{25,17},{2,10},{10... | collective-permute-start | bytes 3145736 | tf_op jit(solution)/shard_map/ppermute | solution.py:13
  24.8 1.5 collective-permute-start.1
  27.1 21.9 %collective-permute-done = bf16[64,8192]{1,0:T(8,128)(2,1)S(1)} collective-permute-done((bf16[64,8192]{1,0:T(8,128)(2,1)}, bf16[64,8192]{1,0:T(8,128)(2,1)S(1)}, u32[]{:S(2)}, u32[]{:S(2)}) %collective-permute-start) | collective-permute-done | bytes 1048608 | tf_op jit(solution)/shard_map/ppermute | solution.py:13
  49.0 23.1 %collective-permute-done.1 = bf16[64,8192]{1,0:T(8,128)(2,1)S(1)} collective-permute-done((bf16[64,8192]{1,0:T(8,128)(2,1)}, bf16[64,8192]{1,0:T(8,128)(2,1)S(1)}, u32[]{:S(2)}, u32[]{:S(2)}) %collective-permute-start.1) | collective-permute-done | bytes 1048608 | tf_op jit(solution)/shard_map/ppermute | solution.py:13
  72.2 1.0 copy-done.8
  73.1 5.9 %fusion.11 = (bf16[64,8192]{1,0:T(8,128)(2,1)}, f32[64,8192]{1,0:T(8,128)S(1)}, bf16[64,8192]{1,0:T(8,128)(2,1)}, f32[64,8192]{1,0:T(8,128)S(1)}) fusion(bf16[64,8192]{1,0:T(8,128)(2,1)} %collective-permute-done.2, bf16[64,8192]{1,0:T(8,128)(2,1)} %copy-done.8, bf16[64,8192]{1,0:T(8,128)(2,1)} %copy-done.7, bf16[4,64,8192]{2,1,0:T(8,128)(2,1)} %bitcast.42, ...), kind=kLoop, calls=%fused_computation.29 | loop fusion | flops 8388608 | bytes 14680068 | tf_op jit(solution)/shard_map/convert_element_type | solution.py:57
  79.0 1.1 fusion.7
  80.1 0.2 copy-done.2
  80.4 31.3 %all_to_all.16 = bf16[64,8,1024]{2,0,1:T(8,128)(2,1)S(1)} all-to-all(bf16[64,8,1024]{2,0,1:T(8,128)(2,1)S(1)} %bitcast.46), channel_id=1, replica_groups=mesh['dp'=4,'mp'=8] {'mp'}, dimensions={1} | all-to-all | bytes 2097152 | tf_op jit(solution)/shard_map/all_to_all | solution.py:49
  111.7 1.5 copy.16
  113.3 0.7 all-gather.5.cloned.1.call-update
  114.0 1.3 collective-permute-start.4
  115.3 1.3 collective-permute-start.5
  116.8 1.5 collective-permute-start.3
  118.2 35.3 %collective-permute-done.4 = bf16[64,8192]{1,0:T(8,128)(2,1)} collective-permute-done((bf16[64,8192]{1,0:T(8,128)(2,1)}, bf16[64,8192]{1,0:T(8,128)(2,1)}, u32[]{:S(2)}, u32[]{:S(2)}) %collective-permute-start.4) | collective-permute-done | bytes 1048608 | tf_op jit(solution)/shard_map/ppermute | solution.py:23
  153.5 1.4 convert_element_type.60
  154.9 21.1 %collective-permute-done.5 = bf16[64,8192]{1,0:T(8,128)(2,1)} collective-permute-done((bf16[64,8192]{1,0:T(8,128)(2,1)}, bf16[64,8192]{1,0:T(8,128)(2,1)}, u32[]{:S(2)}, u32[]{:S(2)}) %collective-permute-start.5) | collective-permute-done | bytes 1048608 | tf_op jit(solution)/shard_map/ppermute | solution.py:23
  176.0 1.4 convert_element_type.62
  177.4 4.0 %fusion.1 = (f32[86,8192]{1,0:T(8,128)}, f32[86,8192]{1,0:T(8,128)}) fusion(s32[]{:T(128)S(6)} %select_n.22, f32[64,8192]{1,0:T(8,128)S(1)} %get-tuple-element.21, f32[64,8192]{1,0:T(8,128)S(1)} %convert_element_type.62, f32[86]{0:T(128)S(1)} %pad_dynamic-slice_fusion.6, f32[64,8192]{1,0:T(8,128)S(1)} %convert_element_type.60, f32[64,8192]{1,0:T(8,128)S(1)} %copy-done.3), kind=kLoop, calls=%fused_computation.9 | loop fusion | flops 2818048 | bytes 14025052 | tf_op jit(solution)/shard_map/concatenate | solution.py:58
  181.3 6.7 %broadcast_in_dim.14 = f32[1,86,8192]{2,0,1:T(1,128)} reshape(f32[86,8192]{1,0:T(8,128)} %get-tuple-element.30) | data formatting | bytes 5636096 | tf_op jit(solution)/shard_map/broadcast_in_dim | solution.py:59
  188.0 4.7 %broadcast_in_dim.15 = f32[1,86,8192]{2,0,1:T(1,128)} reshape(f32[86,8192]{1,0:T(8,128)S(1)} %copy-done.5) | data formatting | bytes 5636096 | tf_op jit(solution)/shard_map/broadcast_in_dim | solution.py:59
  192.8 4.1 %collective-permute-done.3 = bf16[64,8192]{1,0:T(8,128)(2,1)} collective-permute-done((bf16[64,8192]{1,0:T(8,128)(2,1)}, bf16[64,8192]{1,0:T(8,128)(2,1)}, u32[]{:S(2)}, u32[]{:S(2)}) %collective-permute-start.3) | collective-permute-done | bytes 1048608 | tf_op jit(solution)/shard_map/ppermute | solution.py:23
  196.9 3.4 %fusion.10 = bf16[1,86,8192]{2,1,0:T(8,128)(2,1)} fusion(s32[]{:T(128)S(6)} %select_n.22, bf16[64,8192]{1,0:T(8,128)(2,1)} %copy-done.6, bf16[64,8192]{1,0:T(8,128)(2,1)} %collective-permute-done.3, bf16[86]{0:T(256)(128)(2,1)S(1)} %pad_dynamic-slice_fusion.7), kind=kLoop, calls=%fused_computation.22 | loop fusion | flops 4227072 | bytes 3506352 | tf_op jit(solution)/shard_map/broadcast_in_dim | solution.py:59
  200.3 25.5 %all-gather.3.cloned.1.call-done = bf16[8,256,1024]{2,0,1:T(8,128)(2,1)} async-done(((bf16[8,64,1024]{2,0,1:T(8,128)(2,1)}), bf16[8,256,1024]{2,0,1:T(8,128)(2,1)}) %all-gather.3.cloned.1.call-update) | async-done | bytes 4194320 | tf_op jit(solution)/shard_map/all_gather | solution.py:52
  225.8 6.5 %copy.17 = bf16[8,256,1024]{2,1,0:T(8,128)(2,1)} copy(bf16[8,256,1024]{2,0,1:T(8,128)(2,1)} %all-gather.3.cloned.1.call-done) | data formatting | bytes 8388608 | tf_op jit(solution)/shard_map/all_gather | solution.py:52
  232.3 42.9 %all-gather.5.cloned.1.call-done = bf16[1024,2048]{1,0:T(8,128)(2,1)} async-done(((bf16[1024,256]{1,0:T(8,128)(2,1)}), bf16[1024,2048]{1,0:T(8,128)(2,1)}) %all-gather.5.cloned.1.call-update) | async-done | bytes 4194320 | tf_op jit(solution)/shard_map/all_gather | solution.py:33
  275.2 8.3 %convert_bitcast_fusion = bf16[1024,1024]{0,1:T(8,128)(2,1)S(1)} fusion(bf16[2048,1024]{1,0:T(8,128)(2,1)} %bitcast.44, bf16[1024,2048]{1,0:T(8,128)(2,1)} %all-gather.5.cloned.1.call-done), kind=kOutput, calls=%fused_computation.19 | convolution fusion | flops 4296015872 | bytes 10485760 | tf_op jit(solution)/shard_map/dot_general | solution.py:62
  283.5 2.6 copy.18
  (26 shorter events, 0.4 us)
Async XLA Ops:
  7.2 1.1 copy-start
  7.2 218.6 %all-gather.3.cloned.1.call-start = ((), (), s32[]{:S(2)}) async-start(), calls=%async_computation.1 | async-start | bytes 5242880 | tf_op jit(solution)/shard_map/all_gather | solution.py:52
  19.0 2.9 %copy-start.4 = (bf16[256,8192]{1,0:T(8,128)(2,1)}, bf16[256,8192]{1,0:T(8,128)(2,1)S(1)}, u32[]{:S(2)}) copy-start(bf16[256,8192]{1,0:T(8,128)(2,1)S(1)} %convolution_convert_fusion) | copy-start | bytes 12582916
  21.9 27.1 %collective-permute-start = (bf16[64,8192]{1,0:T(8,128)(2,1)}, bf16[64,8192]{1,0:T(8,128)(2,1)S(1)}, u32[]{:S(2)}, u32[]{:S(2)}) collective-permute-start(bf16[64,8192]{1,0:T(8,128)(2,1)} %get-tuple-element.26), channel_id=1, source_target_pairs={{0,8},{8,0},{16,24},{24,16},{1,9},{9,1},{17,25},{25,17},{2,10},{10... | collective-permute-start | bytes 3145736 | tf_op jit(solution)/shard_map/ppermute | solution.py:13
  24.8 47.3 %collective-permute-start.1 = (bf16[64,8192]{1,0:T(8,128)(2,1)}, bf16[64,8192]{1,0:T(8,128)(2,1)S(1)}, u32[]{:S(2)}, u32[]{:S(2)}) collective-permute-start(bf16[64,8192]{1,0:T(8,128)(2,1)} %get-tuple-element.28), channel_id=1, source_target_pairs={{0,16},{8,24},{16,0},{24,8},{1,17},{9,25},{17,1},{25,9},{2,18},{10... | collective-permute-start | bytes 3145736 | tf_op jit(solution)/shard_map/ppermute | solution.py:13
  26.4 46.8 %collective-permute-start.2 = (bf16[64,8192]{1,0:T(8,128)(2,1)}, bf16[64,8192]{1,0:T(8,128)(2,1)}, u32[]{:S(2)}, u32[]{:S(2)}) collective-permute-start(bf16[64,8192]{1,0:T(8,128)(2,1)} %get-tuple-element.27), channel_id=1, source_target_pairs={{0,24},{8,16},{16,8},{24,0},{1,25},{9,17},{17,9},{25,1},{2,26},{10... | collective-permute-start | bytes 3145736 | tf_op jit(solution)/shard_map/ppermute | solution.py:13
  27.1 51.9 %copy-start.9 = (bf16[1,64,8192]{2,1,0:T(8,128)(2,1)S(1)}, bf16[1,64,8192]{2,1,0:T(8,128)(2,1)}, u32[]{:S(2)}) copy-start(bf16[1,64,8192]{2,1,0:T(8,128)(2,1)} %param.9) | copy-start | bytes 3145732
  49.0 23.1 %copy-start.7 = (bf16[64,8192]{1,0:T(8,128)(2,1)}, bf16[64,8192]{1,0:T(8,128)(2,1)S(1)}, u32[]{:S(2)}) copy-start(bf16[64,8192]{1,0:T(8,128)(2,1)S(1)} %collective-permute-done) | copy-start | bytes 3145732
  72.2 1.0 copy-start.8
  79.0 1.3 copy-start.2
  80.3 31.4 %copy-start.6 = (bf16[64,8192]{1,0:T(8,128)(2,1)}, bf16[64,8192]{1,0:T(8,128)(2,1)S(1)}, u32[]{:S(2)}) copy-start(bf16[64,8192]{1,0:T(8,128)(2,1)S(1)} %fusion.7) | copy-start | bytes 3145732
  113.2 162.0 %all-gather.5.cloned.1.call-start = ((), (), s32[]{:S(2)}) async-start(), calls=%async_computation.2 | async-start | bytes 4718592 | tf_op jit(solution)/shard_map/all_gather | solution.py:33
  114.0 39.5 %collective-permute-start.4 = (bf16[64,8192]{1,0:T(8,128)(2,1)}, bf16[64,8192]{1,0:T(8,128)(2,1)}, u32[]{:S(2)}, u32[]{:S(2)}) collective-permute-start(bf16[64,8192]{1,0:T(8,128)(2,1)} %get-tuple-element.24), channel_id=1, source_target_pairs={{8,0},{16,8},{24,16},{9,1},{17,9},{25,17},{10,2},{18,10},{26,18},{... | collective-permute-start | bytes 3145736 | tf_op jit(solution)/shard_map/ppermute | solution.py:23
  115.3 60.7 %collective-permute-start.5 = (bf16[64,8192]{1,0:T(8,128)(2,1)}, bf16[64,8192]{1,0:T(8,128)(2,1)}, u32[]{:S(2)}, u32[]{:S(2)}) collective-permute-start(bf16[64,8192]{1,0:T(8,128)(2,1)} %get-tuple-element.20), channel_id=1, source_target_pairs={{8,0},{16,8},{24,16},{9,1},{17,9},{25,17},{10,2},{18,10},{26,18},{... | collective-permute-start | bytes 3145736 | tf_op jit(solution)/shard_map/ppermute | solution.py:23
  116.8 80.1 %collective-permute-start.3 = (bf16[64,8192]{1,0:T(8,128)(2,1)}, bf16[64,8192]{1,0:T(8,128)(2,1)}, u32[]{:S(2)}, u32[]{:S(2)}) collective-permute-start(bf16[64,8192]{1,0:T(8,128)(2,1)} %copy-done.6), channel_id=1, source_target_pairs={{8,0},{16,8},{24,16},{9,1},{17,9},{25,17},{10,2},{18,10},{26,18},{... | collective-permute-start | bytes 3145736 | tf_op jit(solution)/shard_map/ppermute | solution.py:23
  154.9 22.5 %copy-start.3 = (f32[64,8192]{1,0:T(8,128)S(1)}, f32[64,8192]{1,0:T(8,128)}, u32[]{:S(2)}) copy-start(f32[64,8192]{1,0:T(8,128)} %copy-done.2) | copy-start | bytes 6291460
  181.3 6.7 %copy-start.5 = (f32[86,8192]{1,0:T(8,128)S(1)}, f32[86,8192]{1,0:T(8,128)}, u32[]{:S(2)}) copy-start(f32[86,8192]{1,0:T(8,128)} %get-tuple-element.29) | copy-start | bytes 8454148
  275.2 10.9 %copy-start.1 = (bf16[1024,256]{1,0:T(8,128)(2,1)S(1)}, bf16[1024,256]{1,0:T(8,128)(2,1)}, u32[]{:S(2)}) copy-start(bf16[1024,256]{1,0:T(8,128)(2,1)} %param.7) | copy-start | bytes 1572868
Sparse Core Ops, SparseCore 0:
  113.3 112.3 all-gather.2
  227.4 47.7 all-gather.4
where the time goes:
time: 293 us
  waiting for transfers between devices  175 us (60%)
  blocking collectives  31.3 us (11%)
  local copies, waits for them, and re-layouts  27.4 us (9%)
  matrix products  19 us (6%)
  other arithmetic  17 us (6%)
  between operations  14.9 us (5%)
  starting transfers between devices  8.58 us (3%)
    ppermute x3, waiting for transfers between devices, to_front(): return lax.ppermute(block, axis, [(i, i - 1) for i in range(1, n)])  60.5 us
    ppermute x3, waiting for transfers between devices, exchange(): return lax.ppermute(block, axis, [(i, partner(i, k, n)) for i in range(n)])  45 us
    all_gather x1, waiting for transfers between devices, body(): input_all = lax.all_gather(next_input, 'mp', axis=1, tiled=True)  42.9 us
    all_to_all x1, blocking collectives, body(): lax.all_to_all(new_weight, 'mp', split_axis=1, concat_axis=0, tiled=True)  31.3 us
    all_gather x1, waiting for transfers between devices, body(): weight_cols = lax.all_gather(weight_part, 'dp', axis=1, tiled=True)  25.5 us
    broadcast_in_dim x2, local copies, waits for them, and re-layouts, mine(): return lax.dynamic_slice_in_dim(rows, begin, shard_rows, 0)[None]  11.4 us
    dot_general x1, matrix products, body(): lax.dot_general(activations, out_grad, (((0,), (0,)), ((), ())), preferre...  10.7 us
    convert_element_type x3, other arithmetic, mine(): behind = to_front(block.astype(jnp.bfloat16), 'dp').astype(block.dtype)  8.57 us
  transfers between devices with their start and end apart: 8, of which 7 were waited for; matrix products, arithmetic and copies ran while one was open for 10% of the time, Pallas kernels for 0%

commit v1 on v0

--- a/solution.py
+++ b/solution.py
@@ -30,7 +30,14 @@
     width = old_weight.shape[2]
     held_rows = old_rows * owners
     shard_rows = (held_rows + owners - 2) // (owners - 1)
-    input_all = lax.all_gather(next_input, "mp", axis=1, tiled=True)
+    devices = lax.axis_size("mp")
+    hops = [(i_2, (i_2 + 1) % devices) for i_2 in range(devices)]
+    pieces = [next_input]
+    for stride in range(1, devices):
+        pieces = [lax.ppermute(pieces[0], "mp", hops), *pieces]
+    result = jnp.concatenate(pieces, axis=1)
+    shift = (lax.axis_index("mp") + 1) * pieces[-1].shape[1]
+    input_all = jnp.roll(result, shift, axis=1)
     part = lax.dot_general(
         activations, out_grad, (((0,), (0,)), ((), ())), preferred_element_type=jnp.float32
     ).astype(jnp.bfloat16)

time: 293 us -> 258 us (0.88); the launches traced: 293 us -> 254 us
  waiting for transfers between devices: 175 us -> 140 us
  blocking collectives: 31.3 us -> 0 us
  local copies, waits for them, and re-layouts: 27.4 us -> 50.7 us
  starting transfers between devices: 8.58 us -> 13.9 us
    ppermute x0 -> x7, waiting for transfers between devices: none -> 52.1 us  [body(): pieces = [lax.ppermute(pieces[0], 'mp', hops), *pieces]]
    all_gather x1 -> x0, waiting for transfers between devices: 42.9 us -> none  [body(): input_all = lax.all_gather(next_input, 'mp', axis=1, tiled=True)]
    all_to_all x1 -> x0, blocking collectives: 31.3 us -> none  [body(): lax.all_to_all(new_weight, 'mp', split_axis=1, concat_axis=0, tiled=True)]
    all_gather x1, waiting for transfers between devices: 25.5 us -> 0.01 us  [body(): weight_cols = lax.all_gather(weight_part, 'dp', axis=1, tiled=True)]
    unnamed x21 -> x51, local copies, waits for them, and re-layouts: 5.95 us -> 28.3 us
    ppermute x3, waiting for transfers between devices: 60.5 us -> 42.2 us  [to_front(): return lax.ppermute(block, axis, [(i, i - 1) for i in range(1, n)])]
    all_to_all x0 -> x1, starting transfers between devices: none -> 4.88 us  [body(): lax.all_to_all(new_weight, 'mp', split_axis=1, concat_axis=0, tiled=True)]
  transfers between devices with their start and end apart: 8 -> 15, of which waited for: 7 -> 10; matrix products, arithmetic and copies ran while one was open for 10% -> 21% of each run, Pallas kernels for 0% -> 0%
where the time goes in v1:
time: 258 us; the launch traced here: 254 us
  waiting for transfers between devices  140 us (54%)
  local copies, waits for them, and re-layouts  50.7 us (20%)
  matrix products  18.7 us (7%)
  other arithmetic  15.6 us (6%)
  between operations  15 us (6%)
  starting transfers between devices  13.9 us (5%)
    ppermute x7, waiting for transfers between devices, body(): pieces = [lax.ppermute(pieces[0], 'mp', hops), *pieces]  52.1 us
    ppermute x3, waiting for transfers between devices, exchange(): return lax.ppermute(block, axis, [(i, partner(i, k, n)) for i in range(n)])  45.4 us
    ppermute x3, waiting for transfers between devices, to_front(): return lax.ppermute(block, axis, [(i, i - 1) for i in range(1, n)])  42.2 us
    unnamed x51, local copies, waits for them, and re-layouts  28.3 us
    broadcast_in_dim x2, local copies, waits for them, and re-layouts, mine(): return lax.dynamic_slice_in_dim(rows, begin, shard_rows, 0)[None]  11.3 us
    dot_general x1, matrix products, body(): lax.dot_general(activations, out_grad, (((0,), (0,)), ((), ())), preferre...  10.7 us
    convert_element_type x3, other arithmetic, mine(): behind = to_front(block.astype(jnp.bfloat16), 'dp').astype(block.dtype)  8.57 us
    dot_general x1, matrix products, body(): jnp.dot(input_all, weight_cols, preferred_element_type=jnp.float32)  7.91 us
  transfers between devices with their start and end apart: 15, of which 10 were waited for; matrix products, arithmetic and copies ran while one was open for 21% of the time, Pallas kernels for 0%

profile of v1, /device:TPU:0, one launch (start us, length us, event | category | flops | bytes accessed | tf_op | source)
XLA Modules:
  0.0 253.7 jit_solution(16480160155095478219)
XLA Ops:
  8.2 10.7 %convolution_convert_fusion = bf16[256,8192]{1,0:T(8,128)(2,1)S(1)} fusion(bf16[1024,256]{1,0:T(8,128)(2,1)S(1)} %copy-done, bf16[1024,8192]{1,0:T(8,128)(2,1)} %param.8), kind=kOutput, calls=%fused_computation | convolution fusion | flops 4297064448 | bytes 21495808 | tf_op jit(solution)/shard_map/dot_general | solution.py:41
  19.0 1.9 copy-done.4
  20.9 1.7 dynamic-slice_bitcast_fusion.2
  22.7 2.9 %collective-permute-start = (bf16[64,8192]{1,0:T(8,128)(2,1)}, bf16[64,8192]{1,0:T(8,128)(2,1)S(1)}, u32[]{:S(2)}, u32[]{:S(2)}) collective-permute-start(bf16[64,8192]{1,0:T(8,128)(2,1)} %get-tuple-element.10), channel_id=1, source_target_pairs={{0,8},{8,0},{16,24},{24,16},{1,9},{9,1},{17,25},{25,17},{2,10},{10... | collective-permute-start | bytes 3145736 | tf_op jit(solution)/shard_map/ppermute | solution.py:13
  25.6 1.5 collective-permute-start.2
  27.9 21.9 %collective-permute-done = bf16[64,8192]{1,0:T(8,128)(2,1)S(1)} collective-permute-done((bf16[64,8192]{1,0:T(8,128)(2,1)}, bf16[64,8192]{1,0:T(8,128)(2,1)S(1)}, u32[]{:S(2)}, u32[]{:S(2)}) %collective-permute-start) | collective-permute-done | bytes 1048608 | tf_op jit(solution)/shard_map/ppermute | solution.py:13
  49.8 23.0 %collective-permute-done.2 = bf16[64,8192]{1,0:T(8,128)(2,1)S(1)} collective-permute-done((bf16[64,8192]{1,0:T(8,128)(2,1)}, bf16[64,8192]{1,0:T(8,128)(2,1)S(1)}, u32[]{:S(2)}, u32[]{:S(2)}) %collective-permute-start.2) | collective-permute-done | bytes 1048608 | tf_op jit(solution)/shard_map/ppermute | solution.py:13
  74.2 5.9 %fusion.17 = (bf16[64,8192]{1,0:T(8,128)(2,1)}, f32[64,8192]{1,0:T(8,128)S(1)}, bf16[64,8192]{1,0:T(8,128)(2,1)}, f32[64,8192]{1,0:T(8,128)S(1)}) fusion(bf16[64,8192]{1,0:T(8,128)(2,1)} %copy-done.16, bf16[64,8192]{1,0:T(8,128)(2,1)} %collective-permute-done.1, bf16[64,8192]{1,0:T(8,128)(2,1)} %copy-done.15, bf16[4,64,8192]{2,1,0:T(8,128)(2,1)} %bitcast.39, ...), kind=kLoop, calls=%fused_computation.48 | loop fusion | flops 8388608 | bytes 14680068 | tf_op jit(solution)/shard_map/convert_element_type | solution.py:64
  83.2 4.9 %all-to-all-start = ((bf16[64,8,1024]{2,0,1:T(8,128)(2,1)}), bf16[64,8,1024]{2,0,1:T(8,128)(2,1)}, u32[]{:S(2)}, u32[]{:S(2)}) async-start(bf16[64,8,1024]{2,0,1:T(8,128)(2,1)} %bitcast.42), calls=%async_computation | async-start | bytes 2097152 | tf_op jit(solution)/shard_map/all_to_all | solution.py:56
  88.7 27.1 %collective-permute-done.7 = bf16[1024,256]{1,0:T(8,128)(2,1)S(1)} collective-permute-done((bf16[1024,256]{1,0:T(8,128)(2,1)S(1)}, bf16[1024,256]{1,0:T(8,128)(2,1)S(1)}, u32[]{:S(2)}, u32[]{:S(2)}) %collective-permute-start.7) | collective-permute-done | bytes 524320 | tf_op jit(solution)/shard_map/ppermute | solution.py:37
  119.1 7.8 %collective-permute-done.8 = bf16[1024,256]{1,0:T(8,128)(2,1)S(1)} collective-permute-done((bf16[1024,256]{1,0:T(8,128)(2,1)S(1)}, bf16[1024,256]{1,0:T(8,128)(2,1)S(1)}, u32[]{:S(2)}, u32[]{:S(2)}) %collective-permute-start.8) | collective-permute-done | bytes 524320 | tf_op jit(solution)/shard_map/ppermute | solution.py:37
  127.7 10.5 %collective-permute-done.9 = bf16[1024,256]{1,0:T(8,128)(2,1)} collective-permute-done((bf16[1024,256]{1,0:T(8,128)(2,1)S(1)}, bf16[1024,256]{1,0:T(8,128)(2,1)}, u32[]{:S(2)}, u32[]{:S(2)}) %collective-permute-start.9) | collective-permute-done | bytes 524320 | tf_op jit(solution)/shard_map/ppermute | solution.py:37
  138.2 2.8 %copy.13 = bf16[8,64,1024]{2,0,1:T(8,128)(2,1)} copy(bf16[8,64,1024]{2,1,0:T(8,128)(2,1)} %bitcast.11) | data formatting | bytes 2097152 | tf_op jit(solution)/shard_map/all_to_all | solution.py:56
  141.3 1.4 collective-permute-start.3
  142.7 2.2 collective-permute-done.5
  146.2 32.3 %collective-permute-done.4 = bf16[64,8192]{1,0:T(8,128)(2,1)} collective-permute-done((bf16[64,8192]{1,0:T(8,128)(2,1)}, bf16[64,8192]{1,0:T(8,128)(2,1)}, u32[]{:S(2)}, u32[]{:S(2)}) %collective-permute-start.4) | collective-permute-done | bytes 1048608 | tf_op jit(solution)/shard_map/ppermute | solution.py:23
  180.0 3.9 %fusion.3 = (f32[86,8192]{1,0:T(8,128)}, f32[86,8192]{1,0:T(8,128)}) fusion(s32[]{:T(128)S(6)} %select_n.35, f32[64,8192]{1,0:T(8,128)S(1)} %get-tuple-element.5, f32[64,8192]{1,0:T(8,128)S(1)} %convert_element_type.59, f32[86]{0:T(128)S(1)} %pad_dynamic-slice_fusion.6, f32[64,8192]{1,0:T(8,128)S(1)} %convert_element_type.57, f32[64,8192]{1,0:T(8,128)S(1)} %copy-done.3), kind=kLoop, calls=%fused_computation.11 | loop fusion | flops 2818048 | bytes 14025052 | tf_op jit(solution)/shard_map/concatenate | solution.py:65
  183.9 6.8 %collective-permute-done.11 = bf16[1024,256]{1,0:T(8,128)(2,1)} collective-permute-done((bf16[1024,256]{1,0:T(8,128)(2,1)}, bf16[1024,256]{1,0:T(8,128)(2,1)}, u32[]{:S(2)}, u32[]{:S(2)}) %collective-permute-start.11) | collective-permute-done | bytes 524320 | tf_op jit(solution)/shard_map/ppermute | solution.py:37
  190.7 7.7 %collective-permute-done.3 = bf16[64,8192]{1,0:T(8,128)(2,1)S(1)} collective-permute-done((bf16[64,8192]{1,0:T(8,128)(2,1)}, bf16[64,8192]{1,0:T(8,128)(2,1)S(1)}, u32[]{:S(2)}, u32[]{:S(2)}) %collective-permute-start.3) | collective-permute-done | bytes 1048608 | tf_op jit(solution)/shard_map/ppermute | solution.py:23
  198.5 2.0 fusion.15
  200.5 6.5 %broadcast_in_dim.15 = f32[1,86,8192]{2,0,1:T(1,128)} reshape(f32[86,8192]{1,0:T(8,128)} %get-tuple-element.13) | data formatting | bytes 5636096 | tf_op jit(solution)/shard_map/broadcast_in_dim | solution.py:66
  207.0 4.7 %broadcast_in_dim.14 = f32[1,86,8192]{2,0,1:T(1,128)} reshape(f32[86,8192]{1,0:T(8,128)S(1)} %copy-done.5) | data formatting | bytes 5636096 | tf_op jit(solution)/shard_map/broadcast_in_dim | solution.py:66
  211.8 2.1 constant_dynamic-update-slice_fusion.15
  213.8 1.9 constant_dynamic-update-slice_fusion.14
  215.8 2.0 constant_dynamic-update-slice_fusion.13
  217.7 1.9 constant_dynamic-update-slice_fusion.12
  223.2 1.9 constant_dynamic-update-slice_fusion.7
  225.1 1.9 constant_dynamic-update-slice_fusion.6
  227.1 1.9 constant_dynamic-update-slice_fusion.5
  229.0 1.9 constant_dynamic-update-slice_fusion.4
  234.4 4.5 %copy.14 = bf16[8,256,1024]{2,1,0:T(8,128)(2,1)S(1)} copy(bf16[8,256,1024]{2,0,1:T(8,128)(2,1)} %all-gather.2.cloned.1.call-done) | data formatting | bytes 8388608 | tf_op jit(solution)/shard_map/all_gather | solution.py:59
  239.0 7.9 %fusion.10 = bf16[1024,1024]{1,0:T(8,128)(2,1)} fusion(bf16[2048,1024]{1,0:T(8,128)(2,1)S(1)} %bitcast.41, bf16[1024,4096]{1,0:T(8,128)(2,1)} %constant_dynamic-update-slice_fusion, s32[]{:T(128)S(6)} %select_n.37), kind=kOutput, calls=%fused_computation.21 | convolution fusion | flops 4296015872 | bytes 10485764 | tf_op jit(solution)/shard_map/dot_general | solution.py:69
  (69 shorter events, 20.5 us)
Async XLA Ops:
  7.2 1.1 copy-start
  19.0 2.0 copy-start.4
  19.0 8.2 %copy-start.8 = (bf16[1024,256]{1,0:T(8,128)(2,1)S(1)}, bf16[1024,256]{1,0:T(8,128)(2,1)}, u32[]{:S(2)}) copy-start(bf16[1024,256]{1,0:T(8,128)(2,1)} %param.13) | copy-start | bytes 1572868
  22.7 27.1 %collective-permute-start = (bf16[64,8192]{1,0:T(8,128)(2,1)}, bf16[64,8192]{1,0:T(8,128)(2,1)S(1)}, u32[]{:S(2)}, u32[]{:S(2)}) collective-permute-start(bf16[64,8192]{1,0:T(8,128)(2,1)} %get-tuple-element.10), channel_id=1, source_target_pairs={{0,8},{8,0},{16,24},{24,16},{1,9},{9,1},{17,25},{25,17},{2,10},{10... | collective-permute-start | bytes 3145736 | tf_op jit(solution)/shard_map/ppermute | solution.py:13
  25.6 47.1 %collective-permute-start.2 = (bf16[64,8192]{1,0:T(8,128)(2,1)}, bf16[64,8192]{1,0:T(8,128)(2,1)S(1)}, u32[]{:S(2)}, u32[]{:S(2)}) collective-permute-start(bf16[64,8192]{1,0:T(8,128)(2,1)} %get-tuple-element.11), channel_id=1, source_target_pairs={{0,24},{8,16},{16,8},{24,0},{1,25},{9,17},{17,9},{25,1},{2,26},{10... | collective-permute-start | bytes 3145736 | tf_op jit(solution)/shard_map/ppermute | solution.py:13
  27.1 47.1 %collective-permute-start.1 = (bf16[64,8192]{1,0:T(8,128)(2,1)}, bf16[64,8192]{1,0:T(8,128)(2,1)}, u32[]{:S(2)}, u32[]{:S(2)}) collective-permute-start(bf16[64,8192]{1,0:T(8,128)(2,1)} %get-tuple-element.12), channel_id=1, source_target_pairs={{0,16},{8,24},{16,0},{24,8},{1,17},{9,25},{17,1},{25,9},{2,18},{10... | collective-permute-start | bytes 3145736 | tf_op jit(solution)/shard_map/ppermute | solution.py:13
  27.1 61.0 %collective-permute-start.6 = (bf16[1024,256]{1,0:T(8,128)(2,1)S(1)}, bf16[1024,256]{1,0:T(8,128)(2,1)S(1)}, u32[]{:S(2)}, u32[]{:S(2)}) collective-permute-start(bf16[1024,256]{1,0:T(8,128)(2,1)S(1)} %copy-done.8), channel_id=1, source_target_pairs={{0,1},{1,2},{2,3},{3,4},{4,5},{5,6},{6,7},{7,0},{8,9},{9,10},{10,1... | collective-permute-start | bytes 1572872 | tf_op jit(solution)/shard_map/ppermute | solution.py:37
  27.9 52.2 %copy-start.17 = (bf16[1,64,8192]{2,1,0:T(8,128)(2,1)S(1)}, bf16[1,64,8192]{2,1,0:T(8,128)(2,1)}, u32[]{:S(2)}) copy-start(bf16[1,64,8192]{2,1,0:T(8,128)(2,1)} %param.9) | copy-start | bytes 3145732
  49.8 23.0 %copy-start.15 = (bf16[64,8192]{1,0:T(8,128)(2,1)}, bf16[64,8192]{1,0:T(8,128)(2,1)S(1)}, u32[]{:S(2)}) copy-start(bf16[64,8192]{1,0:T(8,128)(2,1)S(1)} %collective-permute-done) | copy-start | bytes 3145732
  72.8 1.0 copy-start.16
  80.1 3.1 %copy-start.2 = (f32[64,8192]{1,0:T(8,128)}, f32[64,8192]{1,0:T(8,128)S(1)}, u32[]{:S(2)}) copy-start(f32[64,8192]{1,0:T(8,128)S(1)} %get-tuple-element.9) | copy-start | bytes 6291460
  81.2 1.0 copy-start.6
  83.2 55.0 %all-to-all-start = ((bf16[64,8,1024]{2,0,1:T(8,128)(2,1)}), bf16[64,8,1024]{2,0,1:T(8,128)(2,1)}, u32[]{:S(2)}, u32[]{:S(2)}) async-start(bf16[64,8,1024]{2,0,1:T(8,128)(2,1)} %bitcast.42), calls=%async_computation | async-start | bytes 2097152 | tf_op jit(solution)/shard_map/all_to_all | solution.py:56
  88.1 146.3 %all-gather.2.cloned.1.call-start = ((), (), s32[]{:S(2)}) async-start(), calls=%async_computation.1 | async-start | bytes 5242880 | tf_op jit(solution)/shard_map/all_gather | solution.py:59
  88.1 91.8 %copy-start.9 = (bf16[1024,256]{1,0:T(8,128)(2,1)}, bf16[1024,256]{1,0:T(8,128)(2,1)S(1)}, u32[]{:S(2)}) copy-start(bf16[1024,256]{1,0:T(8,128)(2,1)S(1)} %collective-permute-done.6) | copy-start | bytes 1572868
  88.2 27.6 %collective-permute-start.7 = (bf16[1024,256]{1,0:T(8,128)(2,1)S(1)}, bf16[1024,256]{1,0:T(8,128)(2,1)S(1)}, u32[]{:S(2)}, u32[]{:S(2)}) collective-permute-start(bf16[1024,256]{1,0:T(8,128)(2,1)S(1)} %collective-permute-done.6), channel_id=1, source_target_pairs={{0,1},{1,2},{2,3},{3,4},{4,5},{5,6},{6,7},{7,0},{8,9},{9,10},{10,1... | collective-permute-start | bytes 1572872 | tf_op jit(solution)/shard_map/ppermute | solution.py:37
  115.7 0.8 copy-start.11
  116.5 10.4 %collective-permute-start.8 = (bf16[1024,256]{1,0:T(8,128)(2,1)S(1)}, bf16[1024,256]{1,0:T(8,128)(2,1)S(1)}, u32[]{:S(2)}, u32[]{:S(2)}) collective-permute-start(bf16[1024,256]{1,0:T(8,128)(2,1)S(1)} %collective-permute-done.7), channel_id=1, source_target_pairs={{0,1},{1,2},{2,3},{3,4},{4,5},{5,6},{6,7},{7,0},{8,9},{9,10},{10,1... | collective-permute-start | bytes 1572872 | tf_op jit(solution)/shard_map/ppermute | solution.py:37
  116.5 28.3 %collective-permute-start.5 = (bf16[64,8192]{1,0:T(8,128)(2,1)}, bf16[64,8192]{1,0:T(8,128)(2,1)}, u32[]{:S(2)}, u32[]{:S(2)}) collective-permute-start(bf16[64,8192]{1,0:T(8,128)(2,1)} %get-tuple-element.4), channel_id=1, source_target_pairs={{8,0},{16,8},{24,16},{9,1},{17,9},{25,17},{10,2},{18,10},{26,18},{... | collective-permute-start | bytes 3145736 | tf_op jit(solution)/shard_map/ppermute | solution.py:23
  117.8 60.7 %collective-permute-start.4 = (bf16[64,8192]{1,0:T(8,128)(2,1)}, bf16[64,8192]{1,0:T(8,128)(2,1)}, u32[]{:S(2)}, u32[]{:S(2)}) collective-permute-start(bf16[64,8192]{1,0:T(8,128)(2,1)} %get-tuple-element.8), channel_id=1, source_target_pairs={{8,0},{16,8},{24,16},{9,1},{17,9},{25,17},{10,2},{18,10},{26,18},{... | collective-permute-start | bytes 3145736 | tf_op jit(solution)/shard_map/ppermute | solution.py:23
  127.7 10.5 %collective-permute-start.9 = (bf16[1024,256]{1,0:T(8,128)(2,1)S(1)}, bf16[1024,256]{1,0:T(8,128)(2,1)}, u32[]{:S(2)}, u32[]{:S(2)}) collective-permute-start(bf16[1024,256]{1,0:T(8,128)(2,1)S(1)} %collective-permute-done.8), channel_id=1, source_target_pairs={{0,1},{1,2},{2,3},{3,4},{4,5},{5,6},{6,7},{7,0},{8,9},{9,10},{10,1... | collective-permute-start | bytes 1572872 | tf_op jit(solution)/shard_map/ppermute | solution.py:37
  138.2 41.7 %collective-permute-start.10 = (bf16[1024,256]{1,0:T(8,128)(2,1)}, bf16[1024,256]{1,0:T(8,128)(2,1)}, u32[]{:S(2)}, u32[]{:S(2)}) collective-permute-start(bf16[1024,256]{1,0:T(8,128)(2,1)} %collective-permute-done.9), channel_id=1, source_target_pairs={{0,1},{1,2},{2,3},{3,4},{4,5},{5,6},{6,7},{7,0},{8,9},{9,10},{10,1... | collective-permute-start | bytes 1572872 | tf_op jit(solution)/shard_map/ppermute | solution.py:37
  141.1 38.9 %copy-start.3 = (f32[64,8192]{1,0:T(8,128)S(1)}, f32[64,8192]{1,0:T(8,128)}, u32[]{:S(2)}) copy-start(f32[64,8192]{1,0:T(8,128)} %copy-done.2) | copy-start | bytes 6291460
  141.3 57.2 %collective-permute-start.3 = (bf16[64,8192]{1,0:T(8,128)(2,1)}, bf16[64,8192]{1,0:T(8,128)(2,1)S(1)}, u32[]{:S(2)}, u32[]{:S(2)}) collective-permute-start(bf16[64,8192]{1,0:T(8,128)(2,1)} %copy-done.6), channel_id=1, source_target_pairs={{8,0},{16,8},{24,16},{9,1},{17,9},{25,17},{10,2},{18,10},{26,18},{... | collective-permute-start | bytes 3145736 | tf_op jit(solution)/shard_map/ppermute | solution.py:23
  179.9 18.5 %copy-start.7 = (bf16[64,8192]{1,0:T(8,128)(2,1)S(1)}, bf16[64,8192]{1,0:T(8,128)(2,1)}, u32[]{:S(2)}) copy-start(bf16[64,8192]{1,0:T(8,128)(2,1)} %copy-done.6) | copy-start | bytes 3145732
  179.9 10.8 %collective-permute-start.11 = (bf16[1024,256]{1,0:T(8,128)(2,1)}, bf16[1024,256]{1,0:T(8,128)(2,1)}, u32[]{:S(2)}, u32[]{:S(2)}) collective-permute-start(bf16[1024,256]{1,0:T(8,128)(2,1)} %collective-permute-done.10), channel_id=1, source_target_pairs={{0,1},{1,2},{2,3},{3,4},{4,5},{5,6},{6,7},{7,0},{8,9},{9,10},{10,1... | collective-permute-start | bytes 1572872 | tf_op jit(solution)/shard_map/ppermute | solution.py:37
  183.9 23.1 %copy-start.5 = (f32[86,8192]{1,0:T(8,128)S(1)}, f32[86,8192]{1,0:T(8,128)}, u32[]{:S(2)}) copy-start(f32[86,8192]{1,0:T(8,128)} %get-tuple-element.14) | copy-start | bytes 8454148
  190.7 21.1 %collective-permute-start.12 = (bf16[1024,256]{1,0:T(8,128)(2,1)}, bf16[1024,256]{1,0:T(8,128)(2,1)}, u32[]{:S(2)}, u32[]{:S(2)}) collective-permute-start(bf16[1024,256]{1,0:T(8,128)(2,1)} %collective-permute-done.11), channel_id=1, source_target_pairs={{0,1},{1,2},{2,3},{3,4},{4,5},{5,6},{6,7},{7,0},{8,9},{9,10},{10,1... | collective-permute-start | bytes 1572872 | tf_op jit(solution)/shard_map/ppermute | solution.py:37
  211.8 7.9 %copy-start.14 = (bf16[1024,256]{1,0:T(8,128)(2,1)S(1)}, bf16[1024,256]{1,0:T(8,128)(2,1)}, u32[]{:S(2)}) copy-start(bf16[1024,256]{1,0:T(8,128)(2,1)} %copy-done.13) | copy-start | bytes 1572868
  211.8 8.8 %copy-start.12 = (bf16[1024,256]{1,0:T(8,128)(2,1)S(1)}, bf16[1024,256]{1,0:T(8,128)(2,1)}, u32[]{:S(2)}) copy-start(bf16[1024,256]{1,0:T(8,128)(2,1)} %copy-done.11) | copy-start | bytes 1572868
  211.8 9.6 %copy-start.10 = (bf16[1024,256]{1,0:T(8,128)(2,1)S(1)}, bf16[1024,256]{1,0:T(8,128)(2,1)}, u32[]{:S(2)}) copy-start(bf16[1024,256]{1,0:T(8,128)(2,1)} %copy-done.9) | copy-start | bytes 1572868
  238.9 7.9 %copy-start.1 = (bf16[1024,256]{1,0:T(8,128)(2,1)S(1)}, bf16[1024,256]{1,0:T(8,128)(2,1)}, u32[]{:S(2)}) copy-start(bf16[1024,256]{1,0:T(8,128)(2,1)} %param.7) | copy-start | bytes 1572868
  (1 other events, 0.8 us)
Sparse Core Ops, SparseCore 0:
  141.2 91.0 all-gather.1
